TPU v7x, 32 devices: a whole 2x2x4 slice. The times are simulated.
32 devices in a mesh: grp: 2 (over x), exp: 4 (over y, core), base: 4 (over z).
Axes of the slice: x: 2, y: 2, z: 4, core: 2. Of those that a mesh axis runs over, the one named last changes fastest.
Arguments:
- tokens: bfloat16 [512, 7168], P(('grp', 'exp'), 'base'), parts along dimension 0, may hold values from -6 to 6
- expert_ids: int32 [512, 8], P(('grp', 'exp')), parts along dimension 0, may hold values from 0 to 15, all different within a row; in each aligned block of 64 rows (0 to 63, 64 to 127, ...) at most 48 rows name the same one
- gate_q: int32 [512, 8], P(('grp', 'exp')), parts along dimension 0, may hold values from 1 to 65536
- importance: float32 [7168], P('base'), may hold values from 0.5 to 18
- dense_gate: bfloat16 [16, 7168, 1024], P('exp', None, 'base'), may hold values from -0.0625 to 0.0625
- dense_up: bfloat16 [16, 7168, 1024], P('exp', None, 'base'), may hold values from -0.0625 to 0.0625
- dense_down: bfloat16 [16, 1024, 7168], P('exp', None, 'base'), may hold values from -0.1875 to 0.1875
- delta_gate: bfloat16 [16, 7168, 128], P('exp', None, 'base'), may hold values from -0.0625 to 0.0625
- delta_up: bfloat16 [16, 7168, 128], P('exp', None, 'base'), may hold values from -0.0625 to 0.0625
- delta_down: bfloat16 [16, 128, 7168], P('exp', None, 'base'), may hold values from -0.5 to 0.5
- base_gate: bfloat16 [7168, 1024], P(None, 'base'), may hold values from -0.0625 to 0.0625
- base_up: bfloat16 [7168, 1024], P(None, 'base'), may hold values from -0.0625 to 0.0625
- base_down: bfloat16 [1024, 7168], P('base'), may hold values from -0.1875 to 0.1875
Outputs:
- errors: float32 [512], P(('grp', 'exp')), parts along dimension 0
There are 2 independent parts, one for each index of `grp`. A program takes and returns all parts, laid end to end along the dimension named above; an argument that names none is the same for every part. Nothing has to cross between parts.
Inputs may be any that keep to these rules, and one draw needn't show every extreme that they name: `expert_ids`: A token names 8 different experts; among the tokens of one index of exp no expert is named more than 48 times.
All inputs are finite; a program needn't handle non-finite values.
Results may differ from a plain program's by a relative error of at most 0.00064.
Values may be sent and summed in bfloat16 or wider, within the bound.
A program may use at most 256 MiB of HBM per device.

v0:
```python
import jax
import jax.numpy as jnp
from jax import lax
from jax.sharding import PartitionSpec as P

D = 7168


def swiglu(rows, gate_w, up_w):
    gate_pre = jnp.dot(rows, gate_w, preferred_element_type=jnp.float32)
    up_pre = jnp.dot(rows, up_w, preferred_element_type=jnp.float32)
    return (jax.nn.silu(gate_pre) * up_pre).astype(jnp.bfloat16)


def shards(
    tokens,
    expert_ids,
    gate_q,
    importance,
    dense_gate,
    dense_up,
    dense_down,
    delta_gate,
    delta_up,
    delta_down,
    base_gate,
    base_up,
    base_down,
):
    groups = lax.axis_size("exp")
    splits = lax.axis_size("base")
    tok_rows, local_width = tokens.shape
    top_k = expert_ids.shape[1]
    local_experts = dense_gate.shape[0]
    capacity = tok_rows * top_k * 3 // (2 * local_experts * groups)
    dense_width = dense_gate.shape[2]
    low_width = delta_gate.shape[2]
    all_rows = tok_rows * groups
    slots = capacity * groups
    routing = lax.all_gather(
        jnp.concatenate([expert_ids, gate_q], axis=1), "exp", axis=0, tiled=True
    )
    own_rows = lax.all_gather(tokens, "base", axis=1, tiled=True)
    rows = lax.all_gather(own_rows, "exp", axis=0, tiled=True)
    ids, gates = (routing[:, :top_k], routing[:, top_k:])
    first = lax.axis_index("exp") * local_experts
    mine = first + jnp.arange(local_experts, dtype=jnp.int32)
    hit = ids[:, None, :] == mine[None, :, None]
    weight = jnp.sum(jnp.where(hit, gates[:, None, :].astype(jnp.float32), 0.0), axis=2) / 65536.0
    named = jnp.any(hit, axis=2)
    order = jnp.arange(all_rows, dtype=jnp.int32)
    block = order // tok_rows
    before = (block[:, None] == block[None, :]) & (order[None, :] < order[:, None])
    position = jnp.dot(
        before.astype(jnp.bfloat16), named.astype(jnp.bfloat16), preferred_element_type=jnp.float32
    ).astype(jnp.int32)
    slot = jnp.where(named, block[:, None] * capacity + position, -1)
    pick = jnp.arange(slots, dtype=jnp.int32)[None, :, None] == slot.T[:, None, :]
    select = pick.astype(jnp.bfloat16)
    shared = swiglu(own_rows, base_gate, base_up)
    partial_value = jnp.dot(shared, base_down, preferred_element_type=jnp.float32)
    base_own = lax.psum_scatter(
        partial_value.astype(jnp.bfloat16), "base", scatter_dimension=1, tiled=True
    )
    base_all = lax.all_gather(base_own, "exp", axis=0, tiled=True)
    packed = []
    for j in range(local_experts):
        hidden = swiglu(rows, dense_gate[j], dense_up[j])
        low = swiglu(rows, delta_gate[j], delta_up[j])
        both = jnp.concatenate([hidden, low], axis=1)
        packed.append(
            jnp.dot(select[j], both, preferred_element_type=jnp.float32).astype(jnp.bfloat16)
        )
    sent = jnp.stack(packed)
    full = lax.all_gather(sent, "base", axis=0, tiled=False)
    total = jnp.zeros((all_rows,), jnp.float32)
    for j in range(local_experts):
        hid = jnp.concatenate([full[b, j, :, :dense_width] for b in range(splits)], axis=1)
        low = jnp.concatenate([full[b, j, :, dense_width:] for b in range(splits)], axis=1)
        residual = jnp.dot(hid, dense_down[j], preferred_element_type=jnp.float32) - jnp.dot(
            low, delta_down[j], preferred_element_type=jnp.float32
        )
        residual = residual.astype(jnp.bfloat16).astype(jnp.float32)
        base_rows = jnp.dot(select[j], base_all, preferred_element_type=jnp.float32)
        deviation = residual - base_rows
        squares = jnp.sum(importance * deviation * deviation, axis=1)
        back = jnp.sum(jnp.where(pick[j], squares[:, None], 0.0), axis=0)
        total = total + weight[:, j] * back
    total = lax.psum(total / D, ("exp", "base"))
    return lax.dynamic_slice_in_dim(total, lax.axis_index("exp") * tok_rows, tok_rows)


def solution(mesh):
    in_specs = (
        P(("grp", "exp"), "base"),
        P(("grp", "exp"), None),
        P(("grp", "exp"), None),
        P("base"),
        P("exp", None, "base"),
        P("exp", None, "base"),
        P("exp", None, "base"),
        P("exp", None, "base"),
        P("exp", None, "base"),
        P("exp", None, "base"),
        P(None, "base"),
        P(None, "base"),
        P("base", None),
    )
    out_specs = P(("grp", "exp"))
    return jax.shard_map(shards, mesh=mesh, in_specs=in_specs, out_specs=out_specs, check_vma=False)
```

profile of v0, /device:TPU:0, one launch (start us, length us, event | category | flops | bytes accessed | tf_op | source)
XLA Modules:
  0.0 204.3 jit_solution(16887898204992520157)
XLA Ops:
  7.4 23.4 %all_gather.19 = bf16[64,7168]{1,0:T(8,128)(2,1)} all-gather(bf16[64,1792]{1,0:T(8,128)(2,1)} %param.13), channel_id=1, replica_groups=mesh['grp'=2,'exp'=4,'base'=4] {'base'}, dimensions={1}, use_global_device_ids=true | all-gather | bytes 1146880 | tf_op jit(solution)/shard_map/all_gather | solution.py:43
  30.9 3.1 %fusion.206 = f32[64,256]{1,0:T(8,128)S(1)} fusion(bf16[64,7168]{1,0:T(8,128)(2,1)} %all_gather.19, bf16[7168,256]{1,0:T(8,128)(2,1)} %param.23), kind=kOutput, calls=%fused_computation.267 | convolution fusion | flops 234881024 | bytes 4653056 | tf_op jit(solution)/shard_map/dot_general | solution.py:10
  34.0 6.8 %convolution_convert_fusion = bf16[64,7168]{1,0:T(8,128)(2,1)} fusion(bf16[256,7168]{1,0:T(8,128)(2,1)} %param.25, bf16[64,7168]{1,0:T(8,128)(2,1)S(1)} %copy-done.1, bf16[7168,256]{1,0:T(8,128)(2,1)} %param.24, f32[64,256]{1,0:T(8,128)S(1)} %fusion.206), kind=kOutput, calls=%fused_computation | convolution fusion | flops 470319104 | bytes 9240576 | tf_op jit(solution)/shard_map/dot_general | solution.py:61
  40.9 5.5 %all-gather.1 = s32[4,64,16]{1,2,0:T(8,128)S(1)} all-gather(s32[1,64,16]{1,2,0:T(8,128)S(1)} %add_bitcast_fusion), channel_id=1, replica_groups=mesh['grp'=2,'exp'=4,'base'=4] {'exp'}, dimensions={0}, use_global_device_ids=true | all-gather | bytes 20480 | tf_op jit(solution)/shard_map/all_gather | solution.py:40
  46.5 0.1 compare_reduce_fusion
  46.6 0.2 fusion.82
  46.9 0.1 iota_compare_fusion
  47.0 15.2 %all-gather.5.cloned.1.call-done = bf16[256,7168]{1,0:T(8,128)(2,1)} async-done(((bf16[64,7168]{1,0:T(8,128)(2,1)}), bf16[256,7168]{1,0:T(8,128)(2,1)}) %all-gather.5.cloned.1.call-update) | async-done | bytes 3670032 | tf_op jit(solution)/shard_map/all_gather | solution.py:44
  62.2 3.4 %fusion.88 = f32[256,32]{0,1:T(8,128)S(1)} fusion(bf16[256,7168]{1,0:T(8,128)(2,1)} %all-gather.5.cloned.1.call-done, bf16[4,7168,32]{1,2,0:T(8,128)(2,1)S(1)} %copy-done.2), kind=kOutput, calls=%fused_computation.97 | convolution fusion | flops 117440512 | bytes 4161536 | tf_op jit(solution)/shard_map/dot_general | solution.py:10
  65.6 3.8 %fusion.10 = f32[256,256]{0,1:T(8,128)S(1)} fusion(bf16[256,7168]{1,0:T(8,128)(2,1)S(1)} %copy-done, bf16[4,7168,256]{2,1,0:T(8,128)(2,1)} %param.17), kind=kOutput, calls=%fused_computation.11 | convolution fusion | flops 939524096 | bytes 7602176 | tf_op jit(solution)/shard_map/dot_general | solution.py:10
  69.5 1.2 fusion.80
  70.7 3.9 %fusion.60 = bf16[256,256]{0,1:T(8,128)(2,1)S(1)} fusion(bf16[256,7168]{1,0:T(8,128)(2,1)S(1)} %copy-done, bf16[4,7168,256]{2,1,0:T(8,128)(2,1)} %param.18, f32[256,256]{0,1:T(8,128)S(1)} %fusion.10), kind=kOutput, calls=%fused_computation.69 | convolution fusion | flops 939917312 | bytes 7733248 | tf_op jit(solution)/shard_map/dot_general | solution.py:11
  74.6 0.2 fusion.75
  74.8 1.2 fusion.91
  76.0 1.2 fusion.94
  77.2 1.2 fusion.97
  78.5 1.6 fusion.14
  80.1 1.6 fusion.18
  81.7 1.2 fusion.79
  82.9 1.2 fusion.78
  84.2 3.9 %fusion.63 = bf16[256,256]{0,1:T(8,128)(2,1)S(1)} fusion(bf16[256,7168]{1,0:T(8,128)(2,1)S(1)} %copy-done, bf16[4,7168,256]{2,1,0:T(8,128)(2,1)} %param.18, f32[256,256]{0,1:T(8,128)S(1)} %fusion.14), kind=kOutput, calls=%fused_computation.70 | convolution fusion | flops 939917312 | bytes 7733248 | tf_op jit(solution)/shard_map/dot_general | solution.py:11
  88.1 3.7 %fusion.66 = bf16[256,256]{0,1:T(8,128)(2,1)S(1)} fusion(bf16[256,7168]{1,0:T(8,128)(2,1)S(1)} %copy-done, bf16[4,7168,256]{2,1,0:T(8,128)(2,1)} %param.18, f32[256,256]{0,1:T(8,128)S(1)} %fusion.18), kind=kOutput, calls=%fused_computation.71 | convolution fusion | flops 939917312 | bytes 7733248 | tf_op jit(solution)/shard_map/dot_general | solution.py:11
  91.8 0.2 fusion.74
  92.1 0.2 fusion.73
  92.3 1.2 fusion.77
  93.5 1.6 fusion.22
  95.1 3.7 %fusion.69 = bf16[256,256]{0,1:T(8,128)(2,1)S(1)} fusion(bf16[256,7168]{1,0:T(8,128)(2,1)S(1)} %copy-done, bf16[4,7168,256]{2,1,0:T(8,128)(2,1)} %param.18, f32[256,256]{0,1:T(8,128)S(1)} %fusion.22), kind=kOutput, calls=%fused_computation.72 | convolution fusion | flops 939917312 | bytes 7733248 | tf_op jit(solution)/shard_map/dot_general | solution.py:11
  98.9 0.2 fusion.72
  99.1 0.9 pad_maximum_fusion
  100.2 9.8 %all_gather.23 = bf16[256,1792]{1,0:T(8,128)(2,1)S(1)} all-gather(bf16[64,1792]{1,0:T(8,128)(2,1)} %reduce-scatter.2.cloned.1.call-done), channel_id=1, replica_groups=mesh['grp'=2,'exp'=4,'base'=4] {'exp'}, dimensions={0}, use_global_device_ids=true | all-gather | bytes 1146880 | tf_op jit(solution)/shard_map/all_gather | solution.py:65
  110.0 40.2 %all-gather.7.cloned.1.call-done = bf16[16,192,288]{2,1,0:T(8,128)(2,1)} async-done(((bf16[4,192,288]{2,1,0:T(8,128)(2,1)}), bf16[16,192,288]{2,1,0:T(8,128)(2,1)}) %all-gather.7.cloned.1.call-update) | async-done | bytes 1769488 | tf_op jit(solution)/shard_map/all_gather | solution.py:75
  150.2 1.2 slice_bitcast_fusion.39
  151.4 1.7 slice_bitcast_fusion.23
  153.1 3.1 %fusion.4 = f32[192,1792]{1,0:T(8,128)S(1)} fusion(bf16[4,1024,1792]{2,1,0:T(8,128)(2,1)} %param.19, bf16[192,256]{1,0:T(8,128)(2,1)S(1)} %get-tuple-element.34, bf16[192,256]{1,0:T(8,128)(2,1)S(1)} %get-tuple-element.35, bf16[192,256]{1,0:T(8,128)(2,1)S(1)} %get-tuple-element.36, bf16[192,256]{1,0:T(8,128)(2,1)S(1)} %get-tuple-element.25), kind=kOutput, calls=%fused_computation.5 | convolution fusion | flops 706215936 | bytes 5439488 | tf_op jit(solution)/shard_map/dot_general | solution.py:80
  156.2 0.4 fusion.39
  156.7 0.5 fusion.45
  157.1 3.1 %fusion = f32[192,1792]{1,0:T(8,128)S(1)} fusion(bf16[4,1024,1792]{2,1,0:T(8,128)(2,1)} %param.19, bf16[192,256]{1,0:T(8,128)(2,1)S(1)} %get-tuple-element.26, bf16[192,256]{1,0:T(8,128)(2,1)S(1)} %get-tuple-element.27, bf16[192,256]{1,0:T(8,128)(2,1)S(1)} %get-tuple-element.28, bf16[192,256]{1,0:T(8,128)(2,1)S(1)} %get-tuple-element.29), kind=kOutput, calls=%fused_computation.1 | convolution fusion | flops 706215936 | bytes 5439488 | tf_op jit(solution)/shard_map/dot_general | solution.py:80
  160.3 0.4 fusion.43
  160.7 0.5 fusion.47
  161.2 0.9 fusion.2
  162.1 0.4 fusion.41
  162.5 0.5 fusion.46
  163.0 0.9 fusion.6
  163.9 0.4 fusion.37
  164.3 0.5 fusion.44
  164.7 0.2 select_reduce_fusion.3
  165.0 31.3 %psum.7 = f32[256]{0:T(256)S(1)} all-reduce(f32[256]{0:T(256)S(1)} %add_multiply_fusion), channel_id=1, replica_groups=mesh['grp'=2,'exp'=4,'base'=4] {'exp','base'}, use_global_device_ids=true, to_apply=%region_11.12 | all-reduce | flops 256 | bytes 2048 | tf_op jit(solution)/shard_map/psum | solution.py:89
  196.3 0.6 dynamic_slice.3
  (51 shorter events, 0.6 us)
Async XLA Ops:
  7.4 54.8 %all-gather.5.cloned.1.call-start = ((), (), s32[]{:S(2)}) async-start(), calls=%async_computation.1 | async-start | bytes 4587520 | tf_op jit(solution)/shard_map/all_gather | solution.py:44
  30.8 3.2 %copy-start.1 = (bf16[64,7168]{1,0:T(8,128)(2,1)S(1)}, bf16[64,7168]{1,0:T(8,128)(2,1)}, u32[]{:S(2)}) copy-start(bf16[64,7168]{1,0:T(8,128)(2,1)} %all_gather.19) | copy-start | bytes 2752516
  30.8 69.4 %reduce-scatter.2.cloned.1.call-start = ((), (), s32[]{:S(2)}) async-start(), calls=%async_computation.2 | async-start | bytes 1146880 | tf_op jit(solution)/shard_map/reduce_scatter | solution.py:62
  34.0 6.9 %copy-start.6 = (s32[64,8]{0,1:T(8,128)S(1)}, s32[64,8]{0,1:T(8,128)}, u32[]{:S(2)}) copy-start(s32[64,8]{0,1:T(8,128)} %param.15) | copy-start | bytes 6148
  34.0 6.9 %copy-start.7 = (s32[64,8]{0,1:T(8,128)S(1)}, s32[64,8]{0,1:T(8,128)}, u32[]{:S(2)}) copy-start(s32[64,8]{0,1:T(8,128)} %param.14) | copy-start | bytes 6148
  34.0 28.2 %copy-start.2 = (bf16[4,7168,32]{1,2,0:T(8,128)(2,1)S(1)}, bf16[4,7168,32]{1,2,0:T(8,128)(2,1)}, u32[]{:S(2)}) copy-start(bf16[4,7168,32]{1,2,0:T(8,128)(2,1)} %param.20) | copy-start | bytes 5505028
  40.8 109.4 %all-gather.7.cloned.1.call-start = ((), (), s32[]{:S(2)}) async-start(), calls=%async_computation.3 | async-start | bytes 2949120 | tf_op jit(solution)/shard_map/all_gather | solution.py:75
  62.2 3.4 %copy-start = (bf16[256,7168]{1,0:T(8,128)(2,1)S(1)}, bf16[256,7168]{1,0:T(8,128)(2,1)}, u32[]{:S(2)}) copy-start(bf16[256,7168]{1,0:T(8,128)(2,1)} %all-gather.5.cloned.1.call-done) | copy-start | bytes 11010052
  65.6 3.8 %copy-start.3 = (bf16[4,7168,32]{1,2,0:T(8,128)(2,1)S(1)}, bf16[4,7168,32]{1,2,0:T(8,128)(2,1)}, u32[]{:S(2)}) copy-start(bf16[4,7168,32]{1,2,0:T(8,128)(2,1)} %param.21) | copy-start | bytes 5505028
  69.5 9.0 %slice-start = ((s8[14680064]{0:T(1024)(128)(4,1)}), s8[4194304]{0:T(1024)(128)(4,1)S(1)}, s32[]{:S(2)}) async-start(s8[14680064]{0:T(1024)(128)(4,1)} %bitcast.227), calls=%async_computation.4 | async-start | bytes 8388608
  70.7 7.8 %slice-start.1 = ((s8[14680064]{0:T(1024)(128)(4,1)}), s8[4194304]{0:T(1024)(128)(4,1)S(1)}, s32[]{:S(2)}) async-start(s8[14680064]{0:T(1024)(128)(4,1)} %bitcast.227), calls=%async_computation.5 | async-start | bytes 8388608
  70.7 7.8 %slice-start.2 = ((s8[14680064]{0:T(1024)(128)(4,1)}), s8[4194304]{0:T(1024)(128)(4,1)S(1)}, s32[]{:S(2)}) async-start(s8[14680064]{0:T(1024)(128)(4,1)} %bitcast.227), calls=%async_computation.6 | async-start | bytes 8388608
  76.0 2.5 %slice-start.3 = ((s8[14680064]{0:T(1024)(128)(4,1)}), s8[2097152]{0:T(1024)(128)(4,1)S(1)}, s32[]{:S(2)}) async-start(s8[14680064]{0:T(1024)(128)(4,1)} %bitcast.227), calls=%async_computation.7 | async-start | bytes 4194304
  151.4 9.8 %slice-start.4 = ((s8[14680064]{0:T(1024)(128)(4,1)}), s8[2097152]{0:T(1024)(128)(4,1)S(1)}, s32[]{:S(2)}) async-start(s8[14680064]{0:T(1024)(128)(4,1)} %bitcast.229), calls=%async_computation.8 | async-start | bytes 4194304
  153.1 3.1 %copy-start.4 = (bf16[4,128,1792]{2,1,0:T(8,128)(2,1)S(1)}, bf16[4,128,1792]{2,1,0:T(8,128)(2,1)}, u32[]{:S(2)}) copy-start(bf16[4,128,1792]{2,1,0:T(8,128)(2,1)} %param.22) | copy-start | bytes 5505028
  153.1 3.5 %copy-start.5 = (f32[1792]{0:T(1024)S(1)}, f32[1792]{0:T(1024)}, u32[]{:S(2)}) copy-start(f32[1792]{0:T(1024)} %param.16) | copy-start | bytes 21508
  153.1 8.0 %slice-start.5 = ((s8[14680064]{0:T(1024)(128)(4,1)}), s8[4194304]{0:T(1024)(128)(4,1)S(1)}, s32[]{:S(2)}) async-start(s8[14680064]{0:T(1024)(128)(4,1)} %bitcast.229), calls=%async_computation.9 | async-start | bytes 8388608
  156.6 4.5 %slice-start.6 = ((s8[14680064]{0:T(1024)(128)(4,1)}), s8[4194304]{0:T(1024)(128)(4,1)S(1)}, s32[]{:S(2)}) async-start(s8[14680064]{0:T(1024)(128)(4,1)} %bitcast.229), calls=%async_computation.10 | async-start | bytes 8388608
  157.1 4.1 %slice-start.7 = ((s8[14680064]{0:T(1024)(128)(4,1)}), s8[4194304]{0:T(1024)(128)(4,1)S(1)}, s32[]{:S(2)}) async-start(s8[14680064]{0:T(1024)(128)(4,1)} %bitcast.229), calls=%async_computation.11 | async-start | bytes 8388608
Sparse Core Ops, SparseCore 0:
  30.9 31.2 all-gather.4
Sparse Core Ops, SparseCore 1:
  40.9 24.4 reduce-scatter.1
  100.1 50.0 all-gather.6
where the time goes:
time: 205 us; the launch traced here: 204 us
  blocking collectives  70 us (34%)
  matrix products  58.1 us (28%)
  waiting for transfers between devices  55.4 us (27%)
  between operations  15.3 us (7%)
  local copies, waits for them, and re-layouts  3.8 us (2%)
    all_gather x1, waiting for transfers between devices, shards(): full = lax.all_gather(sent, 'base', axis=0, tiled=False)  40.2 us
    psum x1, blocking collectives, shards(): total = lax.psum(total / D, ('exp', 'base'))  31.3 us
    all_gather x1, blocking collectives, shards(): own_rows = lax.all_gather(tokens, 'base', axis=1, tiled=True)  23.4 us
    dot_general x8, matrix products, swiglu(): up_pre = jnp.dot(rows, up_w, preferred_element_type=jnp.float32)  20.1 us
    dot_general x9, matrix products, swiglu(): gate_pre = jnp.dot(rows, gate_w, preferred_element_type=jnp.float32)  18.7 us
    all_gather x1, waiting for transfers between devices, shards(): rows = lax.all_gather(own_rows, 'exp', axis=0, tiled=True)  15.2 us
    all_gather x1, blocking collectives, shards(): base_all = lax.all_gather(base_own, 'exp', axis=0, tiled=True)  9.8 us
    dot_general x4, matrix products, shards(): jnp.dot(hid, dense_down[j], preferred_element_type=jnp.float32)  7.97 us
  transfers between devices with their start and end apart: 3, of which 2 were waited for; matrix products, arithmetic and copies ran while one was open for 24% of the time, Pallas kernels for 0%

commit v1 on v0

--- a/solution.py
+++ b/solution.py
@@ -86,7 +86,7 @@
         squares = jnp.sum(importance * deviation * deviation, axis=1)
         back = jnp.sum(jnp.where(pick[j], squares[:, None], 0.0), axis=0)
         total = total + weight[:, j] * back
-    total = lax.psum(total / D, ("exp", "base"))
+    total = lax.psum(lax.psum(total / D, "base"), "exp")
     return lax.dynamic_slice_in_dim(total, lax.axis_index("exp") * tok_rows, tok_rows)
 
 

time: 205 us -> 189 us (0.922)
  blocking collectives: 70 us -> 54 us
    psum x1 -> x2, blocking collectives: 31.3 us -> 15.2 us  [shards(): total = lax.psum(lax.psum(total / D, 'base'), 'exp')]
  transfers between devices with their start and end apart: 3 -> 3, of which waited for: 2 -> 2; matrix products, arithmetic and copies ran while one was open for 24% -> 26% of each run, Pallas kernels for 0% -> 0%
where the time goes in v1:
time: 189 us; the launch traced here: 188 us
  matrix products  58.2 us (31%)
  waiting for transfers between devices  55.3 us (29%)
  blocking collectives  54 us (29%)
  between operations  15.3 us (8%)
  local copies, waits for them, and re-layouts  3.79 us (2%)
    all_gather x1, waiting for transfers between devices, shards(): full = lax.all_gather(sent, 'base', axis=0, tiled=False)  40.2 us
    all_gather x1, blocking collectives, shards(): own_rows = lax.all_gather(tokens, 'base', axis=1, tiled=True)  23.4 us
    dot_general x8, matrix products, swiglu(): up_pre = jnp.dot(rows, up_w, preferred_element_type=jnp.float32)  20.1 us
    dot_general x9, matrix products, swiglu(): gate_pre = jnp.dot(rows, gate_w, preferred_element_type=jnp.float32)  18.7 us
    psum x2, blocking collectives, shards(): total = lax.psum(lax.psum(total / D, 'base'), 'exp')  15.2 us
    all_gather x1, waiting for transfers between devices, shards(): rows = lax.all_gather(own_rows, 'exp', axis=0, tiled=True)  15.1 us
    all_gather x1, blocking collectives, shards(): base_all = lax.all_gather(base_own, 'exp', axis=0, tiled=True)  9.8 us
    dot_general x4, matrix products, shards(): jnp.dot(hid, dense_down[j], preferred_element_type=jnp.float32)  7.98 us
  transfers between devices with their start and end apart: 3, of which 2 were waited for; matrix products, arithmetic and copies ran while one was open for 26% of the time, Pallas kernels for 0%

profile of v1, /device:TPU:0, one launch (start us, length us, event | category | flops | bytes accessed | tf_op | source)
XLA Modules:
  0.0 188.2 jit_solution(9238779988478849201)
XLA Ops:
  7.4 23.4 %all_gather.19 = bf16[64,7168]{1,0:T(8,128)(2,1)} all-gather(bf16[64,1792]{1,0:T(8,128)(2,1)} %param.13), channel_id=1, replica_groups=mesh['grp'=2,'exp'=4,'base'=4] {'base'}, dimensions={1}, use_global_device_ids=true | all-gather | bytes 1146880 | tf_op jit(solution)/shard_map/all_gather | solution.py:43
  30.9 3.1 %fusion.206 = f32[64,256]{1,0:T(8,128)S(1)} fusion(bf16[64,7168]{1,0:T(8,128)(2,1)} %all_gather.19, bf16[7168,256]{1,0:T(8,128)(2,1)} %param.23), kind=kOutput, calls=%fused_computation.267 | convolution fusion | flops 234881024 | bytes 4653056 | tf_op jit(solution)/shard_map/dot_general | solution.py:10
  34.0 6.8 %convolution_convert_fusion = bf16[64,7168]{1,0:T(8,128)(2,1)} fusion(bf16[256,7168]{1,0:T(8,128)(2,1)} %param.25, bf16[64,7168]{1,0:T(8,128)(2,1)S(1)} %copy-done.1, bf16[7168,256]{1,0:T(8,128)(2,1)} %param.24, f32[64,256]{1,0:T(8,128)S(1)} %fusion.206), kind=kOutput, calls=%fused_computation | convolution fusion | flops 470319104 | bytes 9240576 | tf_op jit(solution)/shard_map/dot_general | solution.py:61
  40.9 5.5 %all-gather.1 = s32[4,64,16]{1,2,0:T(8,128)S(1)} all-gather(s32[1,64,16]{1,2,0:T(8,128)S(1)} %add_bitcast_fusion), channel_id=1, replica_groups=mesh['grp'=2,'exp'=4,'base'=4] {'exp'}, dimensions={0}, use_global_device_ids=true | all-gather | bytes 20480 | tf_op jit(solution)/shard_map/all_gather | solution.py:40
  46.7 0.2 fusion.82
  46.9 0.1 iota_compare_fusion
  47.0 15.1 %all-gather.5.cloned.1.call-done = bf16[256,7168]{1,0:T(8,128)(2,1)} async-done(((bf16[64,7168]{1,0:T(8,128)(2,1)}), bf16[256,7168]{1,0:T(8,128)(2,1)}) %all-gather.5.cloned.1.call-update) | async-done | bytes 3670032 | tf_op jit(solution)/shard_map/all_gather | solution.py:44
  62.1 3.4 %fusion.88 = f32[256,32]{0,1:T(8,128)S(1)} fusion(bf16[256,7168]{1,0:T(8,128)(2,1)} %all-gather.5.cloned.1.call-done, bf16[4,7168,32]{1,2,0:T(8,128)(2,1)S(1)} %copy-done.2), kind=kOutput, calls=%fused_computation.97 | convolution fusion | flops 117440512 | bytes 4161536 | tf_op jit(solution)/shard_map/dot_general | solution.py:10
  65.6 3.8 %fusion.10 = f32[256,256]{0,1:T(8,128)S(1)} fusion(bf16[256,7168]{1,0:T(8,128)(2,1)S(1)} %copy-done, bf16[4,7168,256]{2,1,0:T(8,128)(2,1)} %param.17), kind=kOutput, calls=%fused_computation.11 | convolution fusion | flops 939524096 | bytes 7602176 | tf_op jit(solution)/shard_map/dot_general | solution.py:10
  69.4 1.2 fusion.80
  70.7 3.9 %fusion.60 = bf16[256,256]{0,1:T(8,128)(2,1)S(1)} fusion(bf16[256,7168]{1,0:T(8,128)(2,1)S(1)} %copy-done, bf16[4,7168,256]{2,1,0:T(8,128)(2,1)} %param.18, f32[256,256]{0,1:T(8,128)S(1)} %fusion.10), kind=kOutput, calls=%fused_computation.69 | convolution fusion | flops 939917312 | bytes 7733248 | tf_op jit(solution)/shard_map/dot_general | solution.py:11
  74.5 0.2 fusion.75
  74.8 1.2 fusion.91
  76.0 1.2 fusion.94
  77.2 1.2 fusion.97
  78.5 1.6 fusion.14
  80.1 1.6 fusion.18
  81.7 1.2 fusion.79
  82.9 1.2 fusion.78
  84.1 3.9 %fusion.63 = bf16[256,256]{0,1:T(8,128)(2,1)S(1)} fusion(bf16[256,7168]{1,0:T(8,128)(2,1)S(1)} %copy-done, bf16[4,7168,256]{2,1,0:T(8,128)(2,1)} %param.18, f32[256,256]{0,1:T(8,128)S(1)} %fusion.14), kind=kOutput, calls=%fused_computation.70 | convolution fusion | flops 939917312 | bytes 7733248 | tf_op jit(solution)/shard_map/dot_general | solution.py:11
  88.1 3.7 %fusion.66 = bf16[256,256]{0,1:T(8,128)(2,1)S(1)} fusion(bf16[256,7168]{1,0:T(8,128)(2,1)S(1)} %copy-done, bf16[4,7168,256]{2,1,0:T(8,128)(2,1)} %param.18, f32[256,256]{0,1:T(8,128)S(1)} %fusion.18), kind=kOutput, calls=%fused_computation.71 | convolution fusion | flops 939917312 | bytes 7733248 | tf_op jit(solution)/shard_map/dot_general | solution.py:11
  91.8 0.2 fusion.74
  92.0 0.2 fusion.73
  92.2 1.2 fusion.77
  93.5 1.6 fusion.22
  95.1 3.7 %fusion.69 = bf16[256,256]{0,1:T(8,128)(2,1)S(1)} fusion(bf16[256,7168]{1,0:T(8,128)(2,1)S(1)} %copy-done, bf16[4,7168,256]{2,1,0:T(8,128)(2,1)} %param.18, f32[256,256]{0,1:T(8,128)S(1)} %fusion.22), kind=kOutput, calls=%fused_computation.72 | convolution fusion | flops 939917312 | bytes 7733248 | tf_op jit(solution)/shard_map/dot_general | solution.py:11
  98.8 0.2 fusion.72
  99.0 1.0 pad_maximum_fusion
  100.2 9.8 %all_gather.23 = bf16[256,1792]{1,0:T(8,128)(2,1)S(1)} all-gather(bf16[64,1792]{1,0:T(8,128)(2,1)} %reduce-scatter.2.cloned.1.call-done), channel_id=1, replica_groups=mesh['grp'=2,'exp'=4,'base'=4] {'exp'}, dimensions={0}, use_global_device_ids=true | all-gather | bytes 1146880 | tf_op jit(solution)/shard_map/all_gather | solution.py:65
  110.0 40.2 %all-gather.7.cloned.1.call-done = bf16[16,192,288]{2,1,0:T(8,128)(2,1)} async-done(((bf16[4,192,288]{2,1,0:T(8,128)(2,1)}), bf16[16,192,288]{2,1,0:T(8,128)(2,1)}) %all-gather.7.cloned.1.call-update) | async-done | bytes 1769488 | tf_op jit(solution)/shard_map/all_gather | solution.py:75
  150.1 1.2 slice_bitcast_fusion.39
  151.3 1.7 slice_bitcast_fusion.23
  153.1 3.1 %fusion.4 = f32[192,1792]{1,0:T(8,128)S(1)} fusion(bf16[4,1024,1792]{2,1,0:T(8,128)(2,1)} %param.19, bf16[192,256]{1,0:T(8,128)(2,1)S(1)} %get-tuple-element.34, bf16[192,256]{1,0:T(8,128)(2,1)S(1)} %get-tuple-element.35, bf16[192,256]{1,0:T(8,128)(2,1)S(1)} %get-tuple-element.36, bf16[192,256]{1,0:T(8,128)(2,1)S(1)} %get-tuple-element.25), kind=kOutput, calls=%fused_computation.5 | convolution fusion | flops 706215936 | bytes 5439488 | tf_op jit(solution)/shard_map/dot_general | solution.py:80
  156.2 0.4 fusion.39
  156.6 0.5 fusion.45
  157.1 3.1 %fusion = f32[192,1792]{1,0:T(8,128)S(1)} fusion(bf16[4,1024,1792]{2,1,0:T(8,128)(2,1)} %param.19, bf16[192,256]{1,0:T(8,128)(2,1)S(1)} %get-tuple-element.26, bf16[192,256]{1,0:T(8,128)(2,1)S(1)} %get-tuple-element.27, bf16[192,256]{1,0:T(8,128)(2,1)S(1)} %get-tuple-element.28, bf16[192,256]{1,0:T(8,128)(2,1)S(1)} %get-tuple-element.29), kind=kOutput, calls=%fused_computation.1 | convolution fusion | flops 706215936 | bytes 5439488 | tf_op jit(solution)/shard_map/dot_general | solution.py:80
  160.2 0.4 fusion.43
  160.6 0.5 fusion.47
  161.2 0.9 fusion.2
  162.1 0.4 fusion.41
  162.5 0.5 fusion.46
  163.0 0.9 fusion.6
  163.8 0.4 fusion.37
  164.3 0.5 fusion.44
  164.7 0.2 select_reduce_fusion.3
  164.9 9.6 %psum.14 = f32[256]{0:T(256)S(1)} all-reduce(f32[256]{0:T(256)S(1)} %add_multiply_fusion), channel_id=1, replica_groups=mesh['grp'=2,'exp'=4,'base'=4] {'base'}, use_global_device_ids=true, to_apply=%region_11.12 | all-reduce | flops 256 | bytes 2048 | tf_op jit(solution)/shard_map/psum | solution.py:89
  174.5 5.6 %psum.15 = f32[256]{0:T(256)S(1)} all-reduce(f32[256]{0:T(256)S(1)} %psum.14), channel_id=1, replica_groups=mesh['grp'=2,'exp'=4,'base'=4] {'exp'}, use_global_device_ids=true, to_apply=%region_12.13 | all-reduce | flops 256 | bytes 2048 | tf_op jit(solution)/shard_map/psum | solution.py:89
  180.1 0.6 dynamic_slice.3
  (52 shorter events, 0.7 us)
Async XLA Ops:
  7.4 54.8 %all-gather.5.cloned.1.call-start = ((), (), s32[]{:S(2)}) async-start(), calls=%async_computation.1 | async-start | bytes 4587520 | tf_op jit(solution)/shard_map/all_gather | solution.py:44
  30.8 3.2 %copy-start.1 = (bf16[64,7168]{1,0:T(8,128)(2,1)S(1)}, bf16[64,7168]{1,0:T(8,128)(2,1)}, u32[]{:S(2)}) copy-start(bf16[64,7168]{1,0:T(8,128)(2,1)} %all_gather.19) | copy-start | bytes 2752516
  30.8 69.3 %reduce-scatter.2.cloned.1.call-start = ((), (), s32[]{:S(2)}) async-start(), calls=%async_computation.2 | async-start | bytes 1146880 | tf_op jit(solution)/shard_map/reduce_scatter | solution.py:62
  34.0 6.9 %copy-start.6 = (s32[64,8]{0,1:T(8,128)S(1)}, s32[64,8]{0,1:T(8,128)}, u32[]{:S(2)}) copy-start(s32[64,8]{0,1:T(8,128)} %param.15) | copy-start | bytes 6148
  34.0 6.9 %copy-start.7 = (s32[64,8]{0,1:T(8,128)S(1)}, s32[64,8]{0,1:T(8,128)}, u32[]{:S(2)}) copy-start(s32[64,8]{0,1:T(8,128)} %param.14) | copy-start | bytes 6148
  34.0 28.1 %copy-start.2 = (bf16[4,7168,32]{1,2,0:T(8,128)(2,1)S(1)}, bf16[4,7168,32]{1,2,0:T(8,128)(2,1)}, u32[]{:S(2)}) copy-start(bf16[4,7168,32]{1,2,0:T(8,128)(2,1)} %param.20) | copy-start | bytes 5505028
  40.8 109.3 %all-gather.7.cloned.1.call-start = ((), (), s32[]{:S(2)}) async-start(), calls=%async_computation.3 | async-start | bytes 2949120 | tf_op jit(solution)/shard_map/all_gather | solution.py:75
  62.1 3.4 %copy-start = (bf16[256,7168]{1,0:T(8,128)(2,1)S(1)}, bf16[256,7168]{1,0:T(8,128)(2,1)}, u32[]{:S(2)}) copy-start(bf16[256,7168]{1,0:T(8,128)(2,1)} %all-gather.5.cloned.1.call-done) | copy-start | bytes 11010052
  65.6 3.8 %copy-start.3 = (bf16[4,7168,32]{1,2,0:T(8,128)(2,1)S(1)}, bf16[4,7168,32]{1,2,0:T(8,128)(2,1)}, u32[]{:S(2)}) copy-start(bf16[4,7168,32]{1,2,0:T(8,128)(2,1)} %param.21) | copy-start | bytes 5505028
  69.4 9.0 %slice-start = ((s8[14680064]{0:T(1024)(128)(4,1)}), s8[4194304]{0:T(1024)(128)(4,1)S(1)}, s32[]{:S(2)}) async-start(s8[14680064]{0:T(1024)(128)(4,1)} %bitcast.227), calls=%async_computation.4 | async-start | bytes 8388608
  70.6 7.8 %slice-start.1 = ((s8[14680064]{0:T(1024)(128)(4,1)}), s8[4194304]{0:T(1024)(128)(4,1)S(1)}, s32[]{:S(2)}) async-start(s8[14680064]{0:T(1024)(128)(4,1)} %bitcast.227), calls=%async_computation.5 | async-start | bytes 8388608
  70.7 7.8 %slice-start.2 = ((s8[14680064]{0:T(1024)(128)(4,1)}), s8[4194304]{0:T(1024)(128)(4,1)S(1)}, s32[]{:S(2)}) async-start(s8[14680064]{0:T(1024)(128)(4,1)} %bitcast.227), calls=%async_computation.6 | async-start | bytes 8388608
  76.0 2.5 %slice-start.3 = ((s8[14680064]{0:T(1024)(128)(4,1)}), s8[2097152]{0:T(1024)(128)(4,1)S(1)}, s32[]{:S(2)}) async-start(s8[14680064]{0:T(1024)(128)(4,1)} %bitcast.227), calls=%async_computation.7 | async-start | bytes 4194304
  151.3 9.8 %slice-start.4 = ((s8[14680064]{0:T(1024)(128)(4,1)}), s8[2097152]{0:T(1024)(128)(4,1)S(1)}, s32[]{:S(2)}) async-start(s8[14680064]{0:T(1024)(128)(4,1)} %bitcast.229), calls=%async_computation.8 | async-start | bytes 4194304
  153.1 3.1 %copy-start.4 = (bf16[4,128,1792]{2,1,0:T(8,128)(2,1)S(1)}, bf16[4,128,1792]{2,1,0:T(8,128)(2,1)}, u32[]{:S(2)}) copy-start(bf16[4,128,1792]{2,1,0:T(8,128)(2,1)} %param.22) | copy-start | bytes 5505028
  153.1 3.5 %copy-start.5 = (f32[1792]{0:T(1024)S(1)}, f32[1792]{0:T(1024)}, u32[]{:S(2)}) copy-start(f32[1792]{0:T(1024)} %param.16) | copy-start | bytes 21508
  153.1 8.0 %slice-start.5 = ((s8[14680064]{0:T(1024)(128)(4,1)}), s8[4194304]{0:T(1024)(128)(4,1)S(1)}, s32[]{:S(2)}) async-start(s8[14680064]{0:T(1024)(128)(4,1)} %bitcast.229), calls=%async_computation.9 | async-start | bytes 8388608
  156.6 4.5 %slice-start.6 = ((s8[14680064]{0:T(1024)(128)(4,1)}), s8[4194304]{0:T(1024)(128)(4,1)S(1)}, s32[]{:S(2)}) async-start(s8[14680064]{0:T(1024)(128)(4,1)} %bitcast.229), calls=%async_computation.10 | async-start | bytes 8388608
  157.1 4.1 %slice-start.7 = ((s8[14680064]{0:T(1024)(128)(4,1)}), s8[4194304]{0:T(1024)(128)(4,1)S(1)}, s32[]{:S(2)}) async-start(s8[14680064]{0:T(1024)(128)(4,1)} %bitcast.229), calls=%async_computation.11 | async-start | bytes 8388608
Sparse Core Ops, SparseCore 0:
  30.9 31.1 all-gather.4
Sparse Core Ops, SparseCore 1:
  40.9 24.3 reduce-scatter.1
  100.1 50.0 all-gather.6
